TPU v7x, 256 devices: a whole 4x4x8 slice. The times are simulated.
256 devices in a mesh: dp: 16 (over x, y), ctx: 16 (over z, core).
Axes of the slice: x: 4, y: 4, z: 8, core: 2. Of those that a mesh axis runs over, the one named last changes fastest.
Arguments:
- queries: bfloat16 [524288, 1024], P(('dp', 'ctx')), parts along dimension 0, as said below
- keys: bfloat16 [524288, 128], P(('dp', 'ctx')), parts along dimension 0, as said below
- values: bfloat16 [524288, 128], P(('dp', 'ctx')), parts along dimension 0, may hold values from -6 to 6
- doc_lengths: int32 [1024], P('dp'), parts along dimension 0, may hold values from 1 to 1024, 32768 in all
- tile_owner: int32 [4096], P('dp'), parts along dimension 0, may hold values from 0 to 255, as said below
Outputs:
- attended: bfloat16 [524288, 1024], P(('dp', 'ctx')), parts along dimension 0
There are 16 independent parts, one for each index of `dp`. A program takes and returns all parts, laid end to end along the dimension named above; each array names one. Nothing has to cross between parts.
Inputs may be any that keep to these rules, and one draw needn't show every extreme that they name: `queries`: entries lie within -8 to 8. `keys`: entries lie within -8 to 8. `doc_lengths`: they sum to 32768; the largest is exactly 1024. `tile_owner`: A permutation of the 256 tiles. For owner o, source s and 0 <= j < 1, position o * 16 + s + j holds a tile of the rows that device s holds in the even layout, that is a tile from s * 16 to s * 16 + 15.
All inputs are finite; a program needn't handle non-finite values.
Results may differ from a plain program's by a relative error of at most 0.0037.
Values may be sent and summed in bfloat16 or wider, within the bound.
A program may use at most 128 MiB of HBM per device.

v0:
```python
import functools

import jax
import jax.numpy as jnp
from jax import lax
from jax.experimental import pallas as pl
from jax.experimental.pallas import tpu as pltpu
from jax.sharding import PartitionSpec as P

TILE = 128
DOC_MOST = 1024
DH = 128
MESH = pl.DeviceIdType.MESH
LOG2E = 1.4426950408889634
MASKED = -1e30


def kernel(
    n, tiles, heads, pair, q_hbm, k_hbm, v_hbm, len_ref, owner_ref, out_hbm,
    q_all, k_ext, v_ext, stage, bias, local_sem, halo_send, halo_recv, send_sem, recv_sem,
):
    dp = lax.axis_index("dp")
    me = lax.axis_index("ctx")
    tokens = tiles * TILE
    window = DOC_MOST + TILE
    reach = DOC_MOST // TILE

    loads = [
        pltpu.make_async_copy(q_hbm, q_all, local_sem.at[0]),
        pltpu.make_async_copy(k_hbm, k_ext.at[pl.ds(reach, tiles)], local_sem.at[1]),
        pltpu.make_async_copy(v_hbm, v_ext.at[pl.ds(reach, tiles)], local_sem.at[2]),
    ]
    for load in loads:
        load.start()

    barrier = pltpu.get_barrier_semaphore()
    for step in range(1, n):
        pl.semaphore_signal(
            barrier, inc=1, device_id=(dp, lax.rem(me + step, n)), device_id_type=MESH
        )
    pl.semaphore_wait(barrier, n - 1)

    following = (dp, lax.rem(me + 1, n))
    halos = [
        pltpu.make_async_remote_copy(
            src_ref=src.at[pl.ds(tiles - reach, reach)],
            dst_ref=dst.at[pl.ds(0, reach)],
            send_sem=halo_send.at[at],
            recv_sem=halo_recv.at[at],
            device_id=following,
            device_id_type=MESH,
        )
        for at, (src, dst) in enumerate(((k_hbm, k_ext), (v_hbm, v_ext)))
    ]
    for halo in halos:
        halo.start()

    lane = lax.broadcasted_iota(jnp.int32, (8, 128), 1)

    run, ends = jnp.int32(0), jnp.full((8, 128), 1 << 24, jnp.int32)
    for doc in range(len_ref.shape[0]):
        run = run + len_ref[doc]
        ends = jnp.where(lane == doc, run, ends)
    ends = ends.astype(jnp.float32)[0:1, :]

    for load in loads:
        load.wait()
    for halo in halos:
        halo.wait()

    row_in = lax.broadcasted_iota(jnp.int32, (TILE, 128), 0)
    key_at = lax.broadcasted_iota(jnp.int32, (TILE, window), 1) - DOC_MOST
    row_at = lax.broadcasted_iota(jnp.int32, (TILE, window), 0)

    def target(step):
        j = step // 2
        dz = (4 - (j + 1) // 2) * (1 - 2 * ((j + 1) % 2))
        return ((me // 2 + dz + n // 2) % (n // 2)) * 2 + (me % 2 + 1 + step % 2) % 2

    def remote(step):
        return pltpu.make_async_remote_copy(
            src_ref=stage.at[step],
            dst_ref=out_hbm.at[pl.ds(me * TILE, TILE)],
            send_sem=send_sem.at[step],
            recv_sem=recv_sem.at[step],
            device_id=(dp, target(step)),
            device_id_type=MESH,
        )

    own = pltpu.make_async_copy(
        stage.at[n - 1], out_hbm.at[pl.ds(me * TILE, TILE)], local_sem.at[3]
    )

    def one_tile(step, carry):
        tile = lax.rem(owner_ref[target(step) * n + me], tiles)
        base = (me * tokens + tile * TILE).astype(jnp.float32)
        begin = jnp.max(
            jnp.where(ends <= row_in.astype(jnp.float32) + base, ends, 0.0),
            axis=1, keepdims=True,
        )
        seen = (key_at <= row_at) & (key_at.astype(jnp.float32) + base >= begin)
        bias[...] = jnp.where(seen, 0.0, MASKED)

        for group in range(heads // pair):
            at = [(group * pair + h) * DH for h in range(pair)]
            q = jnp.concatenate([q_all[tile, :, pl.ds(a, DH)] for a in at], axis=0)
            k = jnp.concatenate([k_ext[tile + b] for b in range(reach + 1)], axis=0)
            v = jnp.concatenate([v_ext[tile + b] for b in range(reach + 1)], axis=0)
            scores = lax.dot_general(
                q, k, (((1,), (1,)), ((), ())), preferred_element_type=jnp.float32
            )
            scores = scores * (LOG2E * DH ** -0.5) + jnp.concatenate([bias[...]] * pair, axis=0)
            peak = jnp.max(scores, axis=1, keepdims=True)
            weights = jnp.exp2(scores - peak)
            total = jnp.sum(weights, axis=1, keepdims=True)
            mixed = jnp.dot(weights.astype(jnp.bfloat16), v, preferred_element_type=jnp.float32)
            mixed = (mixed / total).astype(jnp.bfloat16)
            for h, a in enumerate(at):
                stage[step, :, pl.ds(a, DH)] = mixed[h * TILE:(h + 1) * TILE]

        @pl.when(step < n - 1)
        def _():
            remote(step).start()

        return carry

    lax.fori_loop(0, n, one_tile, 0)
    own.start()

    def finish(step, carry):
        remote(step).wait()
        return carry

    lax.fori_loop(0, n - 1, finish, 0)
    own.wait()


def on_device(n, queries, keys, values, doc_lengths, tile_owner):
    tokens, width = queries.shape
    tiles = tokens // TILE
    heads = width // DH
    any_space = pl.BlockSpec(memory_space=pl.ANY)
    smem = pl.BlockSpec(memory_space=pltpu.SMEM)
    return pl.pallas_call(
        functools.partial(kernel, n, tiles, heads, 2),
        out_shape=jax.ShapeDtypeStruct((tokens, width), queries.dtype),
        in_specs=[any_space, any_space, any_space, smem, smem],
        out_specs=any_space,
        scratch_shapes=[
            pltpu.VMEM((tiles, TILE, width), queries.dtype),
            pltpu.VMEM((DOC_MOST // TILE + tiles, TILE, DH), keys.dtype),
            pltpu.VMEM((DOC_MOST // TILE + tiles, TILE, DH), values.dtype),
            pltpu.VMEM((n, TILE, width), queries.dtype),
            pltpu.VMEM((TILE, DOC_MOST + TILE), jnp.float32),
            pltpu.SemaphoreType.DMA((4,)),
            pltpu.SemaphoreType.DMA((2,)),
            pltpu.SemaphoreType.DMA((2,)),
            pltpu.SemaphoreType.DMA((n,)),
            pltpu.SemaphoreType.DMA((n,)),
        ],
        compiler_params=pltpu.CompilerParams(
            collective_id=0, has_side_effects=True, vmem_limit_bytes=48 << 20
        ),
    )(
        queries.reshape(tiles, TILE, width),
        keys.reshape(tiles, TILE, DH),
        values.reshape(tiles, TILE, DH),
        doc_lengths,
        tile_owner,
    )


def solution(mesh):
    return jax.shard_map(
        functools.partial(on_device, mesh.shape["ctx"]),
        mesh=mesh,
        in_specs=(
            P(("dp", "ctx"), None),
            P(("dp", "ctx"), None),
            P(("dp", "ctx"), None),
            P("dp"),
            P("dp"),
        ),
        out_specs=P(("dp", "ctx"), None),
        check_vma=False,
    )
```

profile of v0, /device:TPU:1, one launch (start us, length us, event | category | flops | bytes accessed | tf_op | source)
XLA Modules:
  0.0 114.9 jit_solution(9114551189503670054)
XLA Ops:
  0.0 0.0 copy-start
  0.0 1.0 copy-done
  1.0 0.0 copy-start.1
  1.0 1.0 copy-done.1
  2.1 0.0 copy-start.2
  2.1 0.7 copy-done.2
  2.8 0.0 copy-start.3
  2.8 0.7 copy-done.3
  3.4 109.4 %shard_map.55 = bf16[2048,1024]{1,0:T(8,128)(2,1)S(1)} custom-call(bf16[16,128,1024]{2,1,0:T(8,128)(2,1)} %bitcast.5, bf16[16,128,128]{2,1,0:T(8,128)(2,1)S(1)} %bitcast.3, bf16[16,128,128]{2,1,0:T(8,128)(2,1)S(1)} %bitcast.4, s32[64]{0:T(128)S(1)} %copy-done.3, s32[256]{0:T(256)S(1)} %copy-done.2), custom_call_target="tpu_custom_call" | custom-call | tf_op jit(solution)/shard_map/pallas_call | solution.py:144
  112.8 2.0 %copy.7 = bf16[2048,1024]{1,0:T(8,128)(2,1)} copy(bf16[2048,1024]{1,0:T(8,128)(2,1)S(1)} %shard_map.55) | data formatting | bytes 8388608
Async XLA Ops:
  0.0 1.0 copy-start
  1.0 1.0 copy-start.1
  2.1 0.7 copy-start.2
  2.8 0.7 copy-start.3
where the time goes:
time: 115 us
  Pallas kernels  109 us (95%)
  local copies, waits for them, and re-layouts  5.43 us (5%)
    pallas_call x1, Pallas kernels, on_device(): pl.pallas_call(functools.partial(kernel, n, tiles, heads, 2), out_shape=j...  109 us
    unnamed x9, local copies, waits for them, and re-layouts  5.43 us

commit v1 on v0

v1 whole, which is shorter than its diff:
```python
import functools

import jax
import jax.numpy as jnp
from jax import lax
from jax.experimental import pallas as pl
from jax.experimental.pallas import tpu as pltpu
from jax.sharding import PartitionSpec as P

TILE = 128
DOC_MOST = 1024
DH = 128
MESH = pl.DeviceIdType.MESH
LOG2E = 1.4426950408889634
MASKED = -1e30
ORDER = ((4, 0), (-3, 0), (3, 0), (-2, 0), (2, 0), (-1, 0), (1, 0), (4, 1), (-3, 1), (3, 1), (-2, 1), (2, 1), (-1, 1), (1, 1), (0, 1), (0, 0))


def kernel(
    n, tiles, heads, chunk, q_hbm, k_hbm, v_hbm, len_hbm, owner_hbm, out_hbm,
    q_all, k_ext, v_ext, stage, bias, len_ref, owner_ref, local_sem, halo_send, halo_recv, send_sem, recv_sem,
):
    dp = lax.axis_index("dp")
    me = lax.axis_index("ctx")
    tokens = tiles * TILE
    window = DOC_MOST + TILE
    reach = DOC_MOST // TILE

    loads = [
        pltpu.make_async_copy(len_hbm, len_ref, local_sem.at[3]),
        pltpu.make_async_copy(owner_hbm, owner_ref, local_sem.at[4]),
        pltpu.make_async_copy(q_hbm, q_all, local_sem.at[0]),
        pltpu.make_async_copy(k_hbm, k_ext.at[pl.ds(reach, tiles)], local_sem.at[1]),
        pltpu.make_async_copy(v_hbm, v_ext.at[pl.ds(reach, tiles)], local_sem.at[2]),
    ]
    for load in loads:
        load.start()

    barrier = pltpu.get_barrier_semaphore()
    for step in range(1, n):
        pl.semaphore_signal(
            barrier, inc=1, device_id=(dp, lax.rem(me + step, n)), device_id_type=MESH
        )
    pl.semaphore_wait(barrier, n - 1)

    following = (dp, lax.rem(me + 1, n))
    halos = [
        pltpu.make_async_remote_copy(
            src_ref=src.at[pl.ds(tiles - reach, reach)],
            dst_ref=dst.at[pl.ds(0, reach)],
            send_sem=halo_send.at[at],
            recv_sem=halo_recv.at[at],
            device_id=following,
            device_id_type=MESH,
        )
        for at, (src, dst) in enumerate(((k_hbm, k_ext), (v_hbm, v_ext)))
    ]
    for halo in halos:
        halo.start()

    loads[0].wait()
    lane = lax.broadcasted_iota(jnp.int32, (8, 128), 1)

    run, ends = jnp.int32(0), jnp.full((8, 128), 1 << 24, jnp.int32)
    for doc in range(len_ref.shape[0]):
        run = run + len_ref[doc]
        ends = jnp.where(lane == doc, run, ends)
    ends = ends.astype(jnp.float32)[0:1, :]

    for load in loads[1:]:
        load.wait()
    for halo in halos:
        halo.wait()

    row_in = lax.broadcasted_iota(jnp.int32, (TILE, 128), 0)
    key_at = lax.broadcasted_iota(jnp.int32, (TILE, window), 1) - DOC_MOST
    row_at = lax.broadcasted_iota(jnp.int32, (TILE, window), 0)

    def target(step):
        dz, flip = jnp.int32(ORDER[0][0]), jnp.int32(ORDER[0][1])
        for at, (hops, other) in enumerate(ORDER[1:], 1):
            dz, flip = jnp.where(step == at, hops, dz), jnp.where(step == at, other, flip)
        return ((me // 2 + dz + n // 2) % (n // 2)) * 2 + (me % 2 + flip) % 2

    def remote(step, part, size):
        return pltpu.make_async_remote_copy(
            src_ref=stage.at[step, pl.ds(part, size)],
            dst_ref=out_hbm.at[pl.ds(me * TILE + part, size)],
            send_sem=send_sem.at[step],
            recv_sem=recv_sem.at[step],
            device_id=(dp, target(step)),
            device_id_type=MESH,
        )

    own = pltpu.make_async_copy(
        stage.at[n - 1], out_hbm.at[pl.ds(me * TILE, TILE)], local_sem.at[5]
    )

    def one_tile(step, carry):
        tile = lax.rem(owner_ref[target(step) * n + me], tiles)
        base = (me * tokens + tile * TILE).astype(jnp.float32)
        begin = jnp.max(
            jnp.where(ends <= row_in.astype(jnp.float32) + base, ends, 0.0),
            axis=1, keepdims=True,
        )
        seen = (key_at <= row_at) & (key_at.astype(jnp.float32) + base >= begin)
        bias[...] = jnp.where(seen, 0.0, MASKED)

        k = jnp.concatenate([k_ext[tile + b] for b in range(reach + 1)], axis=0)
        v = jnp.concatenate([v_ext[tile + b] for b in range(reach + 1)], axis=0)
        for part in range(0, TILE, chunk):
            rows = pl.ds(part, chunk)
            q = jnp.concatenate(
                [q_all[tile, rows, pl.ds(h * DH, DH)] for h in range(heads)], axis=0
            )
            scores = lax.dot_general(
                q, k, (((1,), (1,)), ((), ())), preferred_element_type=jnp.float32
            )
            scores = scores * (LOG2E * DH ** -0.5) + jnp.concatenate([bias[rows]] * heads, axis=0)
            peak = jnp.max(scores, axis=1, keepdims=True)
            weights = jnp.exp2(scores - peak)
            total = jnp.sum(weights, axis=1, keepdims=True)
            mixed = jnp.dot(weights.astype(jnp.bfloat16), v, preferred_element_type=jnp.float32)
            mixed = (mixed / total).astype(jnp.bfloat16)
            for h in range(heads):
                stage[step, rows, pl.ds(h * DH, DH)] = mixed[h * chunk:(h + 1) * chunk]

            @pl.when(step < n - 1)
            def _():
                remote(step, part, chunk).start()

        return carry

    lax.fori_loop(0, n, one_tile, 0)
    own.start()

    def finish(step, carry):
        remote(step, 0, TILE).wait()
        return carry

    lax.fori_loop(0, n - 1, finish, 0)
    own.wait()


def on_device(n, queries, keys, values, doc_lengths, tile_owner):
    tokens, width = queries.shape
    tiles = tokens // TILE
    heads = width // DH
    hbm = pl.BlockSpec(memory_space=pltpu.HBM)
    return pl.pallas_call(
        functools.partial(kernel, n, tiles, heads, 32),
        out_shape=pltpu.VMEM((tokens, width), queries.dtype),
        in_specs=[hbm] * 5,
        out_specs=pl.BlockSpec(memory_space=pltpu.VMEM),
        scratch_shapes=[
            pltpu.VMEM((tiles, TILE, width), queries.dtype),
            pltpu.VMEM((DOC_MOST // TILE + tiles, TILE, DH), keys.dtype),
            pltpu.VMEM((DOC_MOST // TILE + tiles, TILE, DH), values.dtype),
            pltpu.VMEM((n, TILE, width), queries.dtype),
            pltpu.VMEM((TILE, DOC_MOST + TILE), jnp.float32),
            pltpu.SMEM(doc_lengths.shape, jnp.int32),
            pltpu.SMEM(tile_owner.shape, jnp.int32),
            pltpu.SemaphoreType.DMA((6,)),
            pltpu.SemaphoreType.DMA((2,)),
            pltpu.SemaphoreType.DMA((2,)),
            pltpu.SemaphoreType.DMA((n,)),
            pltpu.SemaphoreType.DMA((n,)),
        ],
        compiler_params=pltpu.CompilerParams(
            collective_id=0, has_side_effects=True, vmem_limit_bytes=32 << 20
        ),
    )(
        *(
            pltpu.with_memory_space_constraint(array, pltpu.HBM)
            for array in (
                queries.reshape(tiles, TILE, width),
                keys.reshape(tiles, TILE, DH),
                values.reshape(tiles, TILE, DH),
                doc_lengths,
                tile_owner,
            )
        )
    )


def solution(mesh):
    return jax.shard_map(
        functools.partial(on_device, mesh.shape["ctx"]),
        mesh=mesh,
        in_specs=(
            P(("dp", "ctx"), None),
            P(("dp", "ctx"), None),
            P(("dp", "ctx"), None),
            P("dp"),
            P("dp"),
        ),
        out_specs=P(("dp", "ctx"), None),
        check_vma=False,
    )
```

time: 115 us -> 110 us (0.957)
  local copies, waits for them, and re-layouts: 5.43 us -> 2.02 us
    unnamed x9 -> x1, local copies, waits for them, and re-layouts: 5.43 us -> 2.02 us
    pallas_call x1, Pallas kernels: 109 us -> 108 us  [on_device(): pl.pallas_call(functools.partial(kernel, n, tiles, heads, 32), out_shape=...]
where the time goes in v1:
time: 110 us
  Pallas kernels  108 us (98%)
  local copies, waits for them, and re-layouts  2.02 us (2%)
    pallas_call x1, Pallas kernels, on_device(): pl.pallas_call(functools.partial(kernel, n, tiles, heads, 32), out_shape=...  108 us

profile of v1, /device:TPU:1, one launch (start us, length us, event | category | flops | bytes accessed | tf_op | source)
XLA Modules:
  0.0 109.8 jit_solution(3933955810197046332)
XLA Ops:
  0.0 107.8 %shard_map.55 = bf16[2048,1024]{1,0:T(8,128)(2,1)S(1)} custom-call(bf16[16,128,1024]{2,1,0:T(8,128)(2,1)} %bitcast.3, bf16[16,128,128]{2,1,0:T(8,128)(2,1)} %bitcast.4, bf16[16,128,128]{2,1,0:T(8,128)(2,1)} %bitcast.5, s32[64]{0:T(128)} %len_hbm.1, s32[256]{0:T(256)} %owner_hbm.1), custom_call_target="tpu_custom_call" | custom-call | tf_op jit(solution)/shard_map/pallas_call | solution.py:150
  107.8 2.0 %copy.7 = bf16[2048,1024]{1,0:T(8,128)(2,1)} copy(bf16[2048,1024]{1,0:T(8,128)(2,1)S(1)} %shard_map.55) | data formatting | bytes 8388608

commit v2 on v1

--- a/solution.py
+++ b/solution.py
@@ -13,12 +13,15 @@
 MESH = pl.DeviceIdType.MESH
 LOG2E = 1.4426950408889634
 MASKED = -1e30
+RELAYED = 16
+RELAY_STEP = 5
 ORDER = ((4, 0), (-3, 0), (3, 0), (-2, 0), (2, 0), (-1, 0), (1, 0), (4, 1), (-3, 1), (3, 1), (-2, 1), (2, 1), (-1, 1), (1, 1), (0, 1), (0, 0))
 
 
 def kernel(
     n, tiles, heads, chunk, q_hbm, k_hbm, v_hbm, len_hbm, owner_hbm, out_hbm,
-    q_all, k_ext, v_ext, stage, bias, len_ref, owner_ref, local_sem, halo_send, halo_recv, send_sem, recv_sem,
+    q_all, k_ext, v_ext, stage, bias, len_ref, owner_ref, relay, local_sem, halo_send, halo_recv, send_sem, recv_sem,
+    relay_sem,
 ):
     dp = lax.axis_index("dp")
     me = lax.axis_index("ctx")
@@ -70,17 +73,17 @@
     for load in loads[1:]:
         load.wait()
     for halo in halos:
-        halo.wait()
+        halo.wait_recv()
 
     row_in = lax.broadcasted_iota(jnp.int32, (TILE, 128), 0)
     key_at = lax.broadcasted_iota(jnp.int32, (TILE, window), 1) - DOC_MOST
     row_at = lax.broadcasted_iota(jnp.int32, (TILE, window), 0)
 
-    def target(step):
+    def target(source, step):
         dz, flip = jnp.int32(ORDER[0][0]), jnp.int32(ORDER[0][1])
         for at, (hops, other) in enumerate(ORDER[1:], 1):
             dz, flip = jnp.where(step == at, hops, dz), jnp.where(step == at, other, flip)
-        return ((me // 2 + dz + n // 2) % (n // 2)) * 2 + (me % 2 + flip) % 2
+        return ((source // 2 + dz + n // 2) % (n // 2)) * 2 + (source % 2 + flip) % 2
 
     def remote(step, part, size):
         return pltpu.make_async_remote_copy(
@@ -88,16 +91,37 @@
             dst_ref=out_hbm.at[pl.ds(me * TILE + part, size)],
             send_sem=send_sem.at[step],
             recv_sem=recv_sem.at[step],
-            device_id=(dp, target(step)),
+            device_id=(dp, target(me, step)),
             device_id_type=MESH,
         )
+
+    detours = (me // 2) % 2 == 0
+    relays = (me // 2) % 2 == 1
+    direct = TILE - RELAYED
+    to_relay = pltpu.make_async_remote_copy(
+        src_ref=stage.at[0, pl.ds(direct, RELAYED)],
+        dst_ref=relay,
+        send_sem=send_sem.at[0],
+        recv_sem=relay_sem.at[0],
+        device_id=(dp, lax.rem(me + n - 2, n)),
+        device_id_type=MESH,
+    )
+    source = lax.rem(me + 2, n)
+    onward = pltpu.make_async_remote_copy(
+        src_ref=relay,
+        dst_ref=out_hbm.at[pl.ds(source * TILE + direct, RELAYED)],
+        send_sem=relay_sem.at[1],
+        recv_sem=recv_sem.at[0],
+        device_id=(dp, target(source, 0)),
+        device_id_type=MESH,
+    )
 
     own = pltpu.make_async_copy(
         stage.at[n - 1], out_hbm.at[pl.ds(me * TILE, TILE)], local_sem.at[5]
     )
 
     def one_tile(step, carry):
-        tile = lax.rem(owner_ref[target(step) * n + me], tiles)
+        tile = lax.rem(owner_ref[target(me, step) * n + me], tiles)
         base = (me * tokens + tile * TILE).astype(jnp.float32)
         begin = jnp.max(
             jnp.where(ends <= row_in.astype(jnp.float32) + base, ends, 0.0),
@@ -125,14 +149,32 @@
             for h in range(heads):
                 stage[step, rows, pl.ds(h * DH, DH)] = mixed[h * chunk:(h + 1) * chunk]
 
-            @pl.when(step < n - 1)
-            def _():
-                remote(step, part, chunk).start()
+            if part + chunk < TILE:
+                @pl.when(step < n - 1)
+                def _():
+                    remote(step, part, chunk).start()
+            else:
+                @pl.when((step < n - 1) & ((step > 0) | relays))
+                def _():
+                    remote(step, part, chunk).start()
+
+                @pl.when((step == 0) & detours)
+                def _():
+                    if part < direct:
+                        remote(step, part, direct - part).start()
+                    to_relay.start()
+
+        @pl.when((step == RELAY_STEP) & relays)
+        def _():
+            to_relay.wait_recv()
+            onward.start()
 
         return carry
 
     lax.fori_loop(0, n, one_tile, 0)
     own.start()
+    for halo in halos:
+        halo.wait_send()
 
     def finish(step, carry):
         remote(step, 0, TILE).wait()
@@ -140,6 +182,10 @@
 
     lax.fori_loop(0, n - 1, finish, 0)
     own.wait()
+
+    @pl.when(relays)
+    def _():
+        onward.wait_send()
 
 
 def on_device(n, queries, keys, values, doc_lengths, tile_owner):
@@ -160,11 +206,13 @@
             pltpu.VMEM((TILE, DOC_MOST + TILE), jnp.float32),
             pltpu.SMEM(doc_lengths.shape, jnp.int32),
             pltpu.SMEM(tile_owner.shape, jnp.int32),
+            pltpu.VMEM((RELAYED, width), queries.dtype),
             pltpu.SemaphoreType.DMA((6,)),
             pltpu.SemaphoreType.DMA((2,)),
             pltpu.SemaphoreType.DMA((2,)),
             pltpu.SemaphoreType.DMA((n,)),
             pltpu.SemaphoreType.DMA((n,)),
+            pltpu.SemaphoreType.DMA((2,)),
         ],
         compiler_params=pltpu.CompilerParams(
             collective_id=0, has_side_effects=True, vmem_limit_bytes=32 << 20

time: 110 us -> 107 us (0.973)
  Pallas kernels: 108 us -> 105 us
    pallas_call x1, Pallas kernels: 108 us -> 105 us  [on_device(): pl.pallas_call(functools.partial(kernel, n, tiles, heads, 32), out_shape=...]
where the time goes in v2:
time: 107 us
  Pallas kernels  105 us (98%)
  local copies, waits for them, and re-layouts  2.02 us (2%)
    pallas_call x1, Pallas kernels, on_device(): pl.pallas_call(functools.partial(kernel, n, tiles, heads, 32), out_shape=...  105 us

profile of v2, /device:TPU:1, one launch (start us, length us, event | category | flops | bytes accessed | tf_op | source)
XLA Modules:
  0.0 106.7 jit_solution(4722673043942401908)
XLA Ops:
  0.0 104.7 %shard_map.55 = bf16[2048,1024]{1,0:T(8,128)(2,1)S(1)} custom-call(bf16[16,128,1024]{2,1,0:T(8,128)(2,1)} %bitcast.3, bf16[16,128,128]{2,1,0:T(8,128)(2,1)} %bitcast.4, bf16[16,128,128]{2,1,0:T(8,128)(2,1)} %bitcast.5, s32[64]{0:T(128)} %len_hbm.1, s32[256]{0:T(256)} %owner_hbm.1), custom_call_target="tpu_custom_call" | custom-call | tf_op jit(solution)/shard_map/pallas_call | solution.py:196
  104.7 2.0 %copy.7 = bf16[2048,1024]{1,0:T(8,128)(2,1)} copy(bf16[2048,1024]{1,0:T(8,128)(2,1)S(1)} %shard_map.55) | data formatting | bytes 8388608

commit v3 on v2

--- a/solution.py
+++ b/solution.py
@@ -40,10 +40,19 @@
         load.start()
 
     barrier = pltpu.get_barrier_semaphore()
-    for step in range(1, n):
+    for step in sorted(range(1, n), key=lambda step: abs(step - n // 2)):
         pl.semaphore_signal(
             barrier, inc=1, device_id=(dp, lax.rem(me + step, n)), device_id_type=MESH
         )
+    loads[0].wait()
+    lane = lax.broadcasted_iota(jnp.int32, (8, 128), 1)
+
+    run, ends = jnp.int32(0), jnp.full((8, 128), 1 << 24, jnp.int32)
+    for doc in range(len_ref.shape[0]):
+        run = run + len_ref[doc]
+        ends = jnp.where(lane == doc, run, ends)
+    ends = ends.astype(jnp.float32)[0:1, :]
+
     pl.semaphore_wait(barrier, n - 1)
 
     following = (dp, lax.rem(me + 1, n))
@@ -61,19 +70,8 @@
     for halo in halos:
         halo.start()
 
-    loads[0].wait()
-    lane = lax.broadcasted_iota(jnp.int32, (8, 128), 1)
-
-    run, ends = jnp.int32(0), jnp.full((8, 128), 1 << 24, jnp.int32)
-    for doc in range(len_ref.shape[0]):
-        run = run + len_ref[doc]
-        ends = jnp.where(lane == doc, run, ends)
-    ends = ends.astype(jnp.float32)[0:1, :]
-
     for load in loads[1:]:
         load.wait()
-    for halo in halos:
-        halo.wait_recv()
 
     row_in = lax.broadcasted_iota(jnp.int32, (TILE, 128), 0)
     key_at = lax.broadcasted_iota(jnp.int32, (TILE, window), 1) - DOC_MOST
@@ -120,9 +118,11 @@
         stage.at[n - 1], out_hbm.at[pl.ds(me * TILE, TILE)], local_sem.at[5]
     )
 
-    def one_tile(step, carry):
-        tile = lax.rem(owner_ref[target(me, step) * n + me], tiles)
-        base = (me * tokens + tile * TILE).astype(jnp.float32)
+    def tile_of(step):
+        return lax.rem(owner_ref[target(me, step) * n + me], tiles)
+
+    def make_bias(step):
+        base = (me * tokens + tile_of(step) * TILE).astype(jnp.float32)
         begin = jnp.max(
             jnp.where(ends <= row_in.astype(jnp.float32) + base, ends, 0.0),
             axis=1, keepdims=True,
@@ -130,8 +130,12 @@
         seen = (key_at <= row_at) & (key_at.astype(jnp.float32) + base >= begin)
         bias[...] = jnp.where(seen, 0.0, MASKED)
 
+    make_bias(0)
+    halos[0].wait_recv()
+
+    def one_tile(step, carry):
+        tile = tile_of(step)
         k = jnp.concatenate([k_ext[tile + b] for b in range(reach + 1)], axis=0)
-        v = jnp.concatenate([v_ext[tile + b] for b in range(reach + 1)], axis=0)
         for part in range(0, TILE, chunk):
             rows = pl.ds(part, chunk)
             q = jnp.concatenate(
@@ -144,6 +148,12 @@
             peak = jnp.max(scores, axis=1, keepdims=True)
             weights = jnp.exp2(scores - peak)
             total = jnp.sum(weights, axis=1, keepdims=True)
+            if part == 0:
+                @pl.when(step == 0)
+                def _():
+                    halos[1].wait_recv()
+
+            v = jnp.concatenate([v_ext[tile + b] for b in range(reach + 1)], axis=0)
             mixed = jnp.dot(weights.astype(jnp.bfloat16), v, preferred_element_type=jnp.float32)
             mixed = (mixed / total).astype(jnp.bfloat16)
             for h in range(heads):
@@ -169,6 +179,7 @@
             to_relay.wait_recv()
             onward.start()
 
+        make_bias(lax.rem(step + 1, n))
         return carry
 
     lax.fori_loop(0, n, one_tile, 0)
@@ -194,7 +205,7 @@
     heads = width // DH
     hbm = pl.BlockSpec(memory_space=pltpu.HBM)
     return pl.pallas_call(
-        functools.partial(kernel, n, tiles, heads, 32),
+        functools.partial(kernel, n, tiles, heads, 16),
         out_shape=pltpu.VMEM((tokens, width), queries.dtype),
         in_specs=[hbm] * 5,
         out_specs=pl.BlockSpec(memory_space=pltpu.VMEM),

time: 107 us -> 107 us (level)
  no operation moved by 1% of the time
where the time goes in v3:
time: 107 us
  Pallas kernels  104 us (97%)
  local copies, waits for them, and re-layouts  2.02 us (2%)
    pallas_call x1, Pallas kernels, on_device(): pl.pallas_call(functools.partial(kernel, n, tiles, heads, 16), out_shape=...  104 us

profile of v3, /device:TPU:1, one launch (start us, length us, event | category | flops | bytes accessed | tf_op | source)
XLA Modules:
  0.0 106.5 jit_solution(6467389395533984983)
XLA Ops:
  0.0 104.5 %shard_map.55 = bf16[2048,1024]{1,0:T(8,128)(2,1)S(1)} custom-call(bf16[16,128,1024]{2,1,0:T(8,128)(2,1)} %bitcast.3, bf16[16,128,128]{2,1,0:T(8,128)(2,1)} %bitcast.4, bf16[16,128,128]{2,1,0:T(8,128)(2,1)} %bitcast.5, s32[64]{0:T(128)} %len_hbm.1, s32[256]{0:T(256)} %owner_hbm.1), custom_call_target="tpu_custom_call" | custom-call | tf_op jit(solution)/shard_map/pallas_call | solution.py:207
  104.5 2.0 %copy.7 = bf16[2048,1024]{1,0:T(8,128)(2,1)} copy(bf16[2048,1024]{1,0:T(8,128)(2,1)S(1)} %shard_map.55) | data formatting | bytes 8388608
